TPU v7x, 512 devices: a whole 4x4x16 slice. The times are simulated.
512 devices in a mesh: dp: 32 (over z, core), mp: 16 (over y, x).
Axes of the slice: x: 4, y: 4, z: 16, core: 2. Of those that a mesh axis runs over, the one named last changes fastest.
Arguments:
- hidden_codes: int32 [6144, 3584], P('dp', 'mp'), parts along dimension 0, may hold values from -32768 to 32767, as said below
- token_scales: float32 [6144], P('dp'), parts along dimension 0, may hold values from 0.08 to 0.4
- weight_codes: int32 [14336, 1024], P('mp'), may hold values from -32768 to 32767, as said below
- column_scales: float32 [4096], P('mp'), may hold values from 0.0008 to 0.004
Outputs:
- layer_output: bfloat16 [6144, 4096], P('dp', 'mp'), parts along dimension 0
There are 32 independent parts, one for each index of `dp`. A program takes and returns all parts, laid end to end along the dimension named above; an argument that names none is the same for every part. Nothing has to cross between parts.
Inputs may be any that keep to these rules, and one draw needn't show every extreme that they name: `hidden_codes`: each word is u0 + 16 u1 + 256 u2 + 4096 s3 with u0, u1, u2 in 0..15 and s3 in -8..7. `weight_codes`: each word is u0 + 16 u1 + 256 u2 + 4096 s3 with u0, u1, u2 in 0..15 and s3 in -8..7.
All inputs are finite; a program needn't handle non-finite values.
Results may differ from a plain program's by a relative error of at most 0.025.
Values may be sent and summed in bfloat16 or wider, within the bound.
A program may use at most 64 MiB of HBM per device.

v0:
```python
import math

import jax
import jax.numpy as jnp
import numpy as np
from jax import lax
from jax.sharding import PartitionSpec as P

HC = 28
FF = 14336


def partner_2(value, axis, distance):
    mask = 2**distance
    pairs = [(source, source ^ mask) for source in range(lax.axis_size(axis))]
    return lax.ppermute(value, axis, pairs)


def paley_table():
    modulus = 13
    residues = set((value * value % modulus for value in range(1, modulus)))
    symbols = np.array([0.0] + [1.0 if value in residues else -1.0 for value in range(1, modulus)])
    indices = np.arange(modulus)
    jacobsthal = symbols[(indices[None, :] - indices[:, None]) % modulus]
    first_row = np.concatenate([np.zeros((1, 1)), np.ones((1, modulus))], axis=1)
    other_rows = np.concatenate([np.ones((modulus, 1)), jacobsthal], axis=1)
    conference = np.concatenate([first_row, other_rows], axis=0)
    return np.kron(conference, np.array([[1.0, 1.0], [1.0, -1.0]])) + np.kron(
        np.eye(modulus + 1), np.array([[1.0, -1.0], [-1.0, -1.0]])
    )


def sylvester_table(length):
    indices = np.arange(length)
    intersection = indices[:, None] & indices[None, :]
    parity = intersection & 1
    for shift in range(1, max(length, 2).bit_length()):
        parity = parity ^ intersection >> shift & 1
    return 1.0 - 2.0 * parity


def unpack_words(packed):
    return [packed % 16 - 8, packed // 16 % 16 - 8, packed // 256 % 16 - 8, packed // 4096]


def local_table(block_count, word_count):
    product_table = np.kron(sylvester_table(block_count), paley_table())
    row_order = (4 * np.arange(word_count)[None, :] + np.arange(4)[:, None]).reshape(-1)
    return product_table[row_order, :]


def on_device(hidden_codes, token_scales, weight_codes, column_scales):
    device_count = lax.axis_size("mp")
    word_count = hidden_codes.shape[1]
    local_units = 4 * word_count
    block_count = local_units // HC
    codes = jnp.concatenate(unpack_words(hidden_codes), axis=1)
    hidden = (codes.astype(jnp.float32) * token_scales[:, None]).astype(jnp.bfloat16)
    rotation = jnp.asarray(local_table(block_count, word_count), jnp.bfloat16)
    mixed = jnp.dot(hidden, rotation, preferred_element_type=jnp.float32)
    device_index = lax.axis_index("mp")
    for bit in range(device_count.bit_length() - 1):
        partner = partner_2(mixed.astype(jnp.bfloat16), "mp", bit).astype(mixed.dtype)
        upper = (device_index >> bit & 1).astype(jnp.float32)
        mixed = partner + (1.0 - 2.0 * upper) * mixed
    rotated = (mixed * (1.0 / math.sqrt(FF))).astype(jnp.bfloat16)
    weights = jnp.concatenate(unpack_words(weight_codes), axis=1).astype(jnp.bfloat16)
    partial_term = jnp.dot(rotated, weights, preferred_element_type=jnp.float32)
    summed = lax.psum_scatter(
        partial_term.astype(jnp.bfloat16), "mp", scatter_dimension=1, tiled=True
    ).astype(jnp.float32)
    return (summed * column_scales[None, :]).astype(jnp.bfloat16)


def solution(mesh):
    return jax.shard_map(
        on_device,
        mesh=mesh,
        in_specs=(P("dp", "mp"), P("dp"), P("mp", None), P("mp")),
        out_specs=P("dp", "mp"),
        check_vma=False,
    )
```

profile of v0, /device:TPU:2, one launch (start us, length us, event | category | flops | bytes accessed | tf_op | source)
XLA Modules:
  0.0 169.0 jit_solution(2314851976038347430)
XLA Ops:
  6.5 0.0 reduce-scatter.2.cloned.1.call-start
  6.5 1.4 fusion.34
  7.9 2.1 %fusion.48 = (bf16[192,896]{1,0:T(8,128)(2,1)S(1)}, f32[192,896]{1,0:T(8,128)S(1)}) fusion(bf16[896,896]{1,0:T(8,128)(2,1)} %constant.128.clone, s32[192,224]{1,0:T(8,128)S(1)} %get-tuple-element.14, s32[192,224]{1,0:T(8,128)S(1)} %get-tuple-element.12, s32[192,224]{1,0:T(8,128)S(1)} %get-tuple-element.13, s32[192,224]{1,0:T(8,128)S(1)} %get-tuple-element.11, ...), kind=kOutput, calls=%fused_computation.87 | convolution fusion | flops 309485568 | bytes 3326720 | tf_op jit(solution)/shard_map/dot_general | solution.py:60
  10.0 7.8 %collective-permute-start = (bf16[192,896]{1,0:T(8,128)(2,1)S(1)}, bf16[192,896]{1,0:T(8,128)(2,1)S(1)}, u32[]{:S(2)}, u32[]{:S(2)}) collective-permute-start(bf16[192,896]{1,0:T(8,128)(2,1)S(1)} %get-tuple-element.15), channel_id=1, source_target_pairs={{0,1},{1,0},{2,3},{3,2},{4,5},{5,4},{6,7},{7,6},{8,9},{9,8},{10,11... | collective-permute-start | bytes 1032200 | tf_op jit(solution)/shard_map/ppermute | solution.py:16
  17.9 5.2 %collective-permute-done = bf16[192,896]{1,0:T(8,128)(2,1)S(1)} collective-permute-done((bf16[192,896]{1,0:T(8,128)(2,1)S(1)}, bf16[192,896]{1,0:T(8,128)(2,1)S(1)}, u32[]{:S(2)}, u32[]{:S(2)}) %collective-permute-start) | collective-permute-done | bytes 344096 | tf_op jit(solution)/shard_map/ppermute | solution.py:16
  23.1 0.1 fusion.27
  23.2 2.7 %collective-permute-start.1 = (bf16[192,896]{1,0:T(8,128)(2,1)S(1)}, bf16[192,896]{1,0:T(8,128)(2,1)S(1)}, u32[]{:S(2)}, u32[]{:S(2)}) collective-permute-start(bf16[192,896]{1,0:T(8,128)(2,1)S(1)} %fusion.27), channel_id=1, source_target_pairs={{0,2},{1,3},{2,0},{3,1},{4,6},{5,7},{6,4},{7,5},{8,10},{9,11},{10,... | collective-permute-start | bytes 1032200 | tf_op jit(solution)/shard_map/ppermute | solution.py:16
  25.9 7.9 %collective-permute-done.1 = bf16[192,896]{1,0:T(8,128)(2,1)S(1)} collective-permute-done((bf16[192,896]{1,0:T(8,128)(2,1)S(1)}, bf16[192,896]{1,0:T(8,128)(2,1)S(1)}, u32[]{:S(2)}, u32[]{:S(2)}) %collective-permute-start.1) | collective-permute-done | bytes 344096 | tf_op jit(solution)/shard_map/ppermute | solution.py:16
  33.8 0.1 fusion.47
  34.0 3.8 %collective-permute-start.2 = (bf16[192,896]{1,0:T(8,128)(2,1)S(1)}, bf16[192,896]{1,0:T(8,128)(2,1)S(1)}, u32[]{:S(2)}, u32[]{:S(2)}) collective-permute-start(bf16[192,896]{1,0:T(8,128)(2,1)S(1)} %get-tuple-element.5), channel_id=1, source_target_pairs={{0,4},{1,5},{2,6},{3,7},{4,0},{5,1},{6,2},{7,3},{8,12},{9,13},{10,... | collective-permute-start | bytes 1032200 | tf_op jit(solution)/shard_map/ppermute | solution.py:16
  37.8 6.2 %collective-permute-done.2 = bf16[192,896]{1,0:T(8,128)(2,1)S(1)} collective-permute-done((bf16[192,896]{1,0:T(8,128)(2,1)S(1)}, bf16[192,896]{1,0:T(8,128)(2,1)S(1)}, u32[]{:S(2)}, u32[]{:S(2)}) %collective-permute-start.2) | collective-permute-done | bytes 344096 | tf_op jit(solution)/shard_map/ppermute | solution.py:16
  44.1 0.1 fusion.28
  44.1 5.3 %collective-permute-start.3 = (bf16[192,896]{1,0:T(8,128)(2,1)S(1)}, bf16[192,896]{1,0:T(8,128)(2,1)S(1)}, u32[]{:S(2)}, u32[]{:S(2)}) collective-permute-start(bf16[192,896]{1,0:T(8,128)(2,1)S(1)} %fusion.28), channel_id=1, source_target_pairs={{0,8},{1,9},{2,10},{3,11},{4,12},{5,13},{6,14},{7,15},{8,0},{9,1},... | collective-permute-start | bytes 1032200 | tf_op jit(solution)/shard_map/ppermute | solution.py:16
  49.4 12.3 %fusion.12 = (bf16[896,1024]{1,0:T(8,128)(2,1)S(1)}, bf16[896,1024]{1,0:T(8,128)(2,1)}, bf16[896,1024]{1,0:T(8,128)(2,1)}, bf16[896,1024]{1,0:T(8,128)(2,1)}) fusion(s32[896,1024]{1,0:T(8,128)} %param.7), kind=kLoop, calls=%fused_computation.27 | loop fusion | flops 62390272 | bytes 11010048 | tf_op jit(solution)/shard_map/convert
  61.8 0.0 collective-permute-done.3
  61.8 0.0 copy-start
  61.8 7.7 %fusion.8 = bf16[192,4096]{1,0:T(8,128)(2,1)} fusion(bf16[896,1024]{1,0:T(8,128)(2,1)} %get-tuple-element.10, bf16[896,1024]{1,0:T(8,128)(2,1)} %get-tuple-element.8, bf16[896,1024]{1,0:T(8,128)(2,1)} %get-tuple-element.9, bf16[896,1024]{1,0:T(8,128)(2,1)S(1)} %get-tuple-element.7, bf16[192,896]{1,0:T(8,128)(2,1)S(1)} %collective-permute-done.3, ...), kind=kOutput, calls=%fused_computation.25 | convolution fusion | flops 1440808960 | bytes 10289160 | tf_op jit(solution)/shard_map/dot_general | solution.py:68
  69.5 0.0 reduce-scatter.2.cloned.1.call-update
  69.5 91.1 %reduce-scatter.2.cloned.1.call-done = bf16[192,256]{1,0:T(8,128)(2,1)} async-done(((bf16[192,4096]{1,0:T(8,128)(2,1)}), bf16[192,256]{1,0:T(8,128)(2,1)}) %reduce-scatter.2.cloned.1.call-update) | async-done | bytes 98320 | tf_op jit(solution)/shard_map/reduce_scatter | solution.py:69
  160.6 0.0 copy-done
  160.6 1.6 multiply_convert_fusion.2
Async XLA Ops:
  6.5 154.0 %reduce-scatter.2.cloned.1.call-start = ((), (), s32[]{:S(2)}) async-start(), calls=%async_computation.1 | async-start | bytes 1671168 | tf_op jit(solution)/shard_map/reduce_scatter | solution.py:69
  10.0 13.0 %collective-permute-start = (bf16[192,896]{1,0:T(8,128)(2,1)S(1)}, bf16[192,896]{1,0:T(8,128)(2,1)S(1)}, u32[]{:S(2)}, u32[]{:S(2)}) collective-permute-start(bf16[192,896]{1,0:T(8,128)(2,1)S(1)} %get-tuple-element.15), channel_id=1, source_target_pairs={{0,1},{1,0},{2,3},{3,2},{4,5},{5,4},{6,7},{7,6},{8,9},{9,8},{10,11... | collective-permute-start | bytes 1032200 | tf_op jit(solution)/shard_map/ppermute | solution.py:16
  23.2 10.6 %collective-permute-start.1 = (bf16[192,896]{1,0:T(8,128)(2,1)S(1)}, bf16[192,896]{1,0:T(8,128)(2,1)S(1)}, u32[]{:S(2)}, u32[]{:S(2)}) collective-permute-start(bf16[192,896]{1,0:T(8,128)(2,1)S(1)} %fusion.27), channel_id=1, source_target_pairs={{0,2},{1,3},{2,0},{3,1},{4,6},{5,7},{6,4},{7,5},{8,10},{9,11},{10,... | collective-permute-start | bytes 1032200 | tf_op jit(solution)/shard_map/ppermute | solution.py:16
  34.0 10.1 %collective-permute-start.2 = (bf16[192,896]{1,0:T(8,128)(2,1)S(1)}, bf16[192,896]{1,0:T(8,128)(2,1)S(1)}, u32[]{:S(2)}, u32[]{:S(2)}) collective-permute-start(bf16[192,896]{1,0:T(8,128)(2,1)S(1)} %get-tuple-element.5), channel_id=1, source_target_pairs={{0,4},{1,5},{2,6},{3,7},{4,0},{5,1},{6,2},{7,3},{8,12},{9,13},{10,... | collective-permute-start | bytes 1032200 | tf_op jit(solution)/shard_map/ppermute | solution.py:16
  44.1 17.6 %collective-permute-start.3 = (bf16[192,896]{1,0:T(8,128)(2,1)S(1)}, bf16[192,896]{1,0:T(8,128)(2,1)S(1)}, u32[]{:S(2)}, u32[]{:S(2)}) collective-permute-start(bf16[192,896]{1,0:T(8,128)(2,1)S(1)} %fusion.28), channel_id=1, source_target_pairs={{0,8},{1,9},{2,10},{3,11},{4,12},{5,13},{6,14},{7,15},{8,0},{9,1},... | collective-permute-start | bytes 1032200 | tf_op jit(solution)/shard_map/ppermute | solution.py:16
  61.8 98.8 %copy-start = (f32[256]{0:T(256)S(1)}, f32[256]{0:T(256)}, u32[]{:S(2)}) copy-start(f32[256]{0:T(256)} %param.8) | copy-start | bytes 3076
Sparse Core Ops, SparseCore 0:
  69.6 90.8 reduce-scatter.1
where the time goes:
time: 169 us
  waiting for transfers between devices  110 us (65%)
  starting transfers between devices  19.6 us (12%)
  other arithmetic  15.6 us (9%)
  between operations  13.5 us (8%)
  matrix products  9.81 us (6%)
    reduce_scatter x1, waiting for transfers between devices, on_device(): lax.psum_scatter(partial_term.astype(jnp.bfloat16), 'mp', scatter_dimensi...  91.1 us
    ppermute x4, starting transfers between devices, partner_2(): return lax.ppermute(value, axis, pairs)  19.6 us
    ppermute x4, waiting for transfers between devices, partner_2(): return lax.ppermute(value, axis, pairs)  19.4 us
    another operation x1, other arithmetic  12.3 us
    dot_general x1, matrix products, on_device(): partial_term = jnp.dot(rotated, weights, preferred_element_type=jnp.float32)  7.72 us
  transfers between devices with their start and end apart: 5, of which 4 were waited for; matrix products, arithmetic and copies ran while one was open for 7% of the time, Pallas kernels for 0%

commit v1 on v0

v1 whole, which is shorter than its diff:
```python
import math

import jax
import jax.numpy as jnp
import numpy as np
from jax import lax
from jax.experimental import pallas as pl
from jax.experimental.pallas import tpu as pltpu
from jax.sharding import PartitionSpec as P

HC = 28
FF = 14336
SIDE = 4
N_MP = 16
T = 192
WORDS = 224
WIDE = 256
UNITS = 896
SLICE = 48
HALF = 128
F32 = jnp.float32
BF16 = jnp.bfloat16
MESH = pl.DeviceIdType.MESH

OFFSETS = sorted(
    [(dy, dx) for dy in range(SIDE) for dx in range(SIDE)],
    key=lambda o: -(min(o[0], SIDE - o[0]) + min(o[1], SIDE - o[1])),
)
PEERS = [o for o in OFFSETS if o != (0, 0)]
ORDER = [
    (2, 2), (2, 1), (2, 3), (1, 2), (3, 2), (2, 0), (0, 2), (1, 1),
    (1, 3), (3, 1), (3, 3), (1, 0), (0, 1), (3, 0), (0, 3), (0, 0),
]


def paley_table():
    modulus = 13
    residues = set((value * value % modulus for value in range(1, modulus)))
    symbols = np.array([0.0] + [1.0 if value in residues else -1.0 for value in range(1, modulus)])
    indices = np.arange(modulus)
    jacobsthal = symbols[(indices[None, :] - indices[:, None]) % modulus]
    first_row = np.concatenate([np.zeros((1, 1)), np.ones((1, modulus))], axis=1)
    other_rows = np.concatenate([np.ones((modulus, 1)), jacobsthal], axis=1)
    conference = np.concatenate([first_row, other_rows], axis=0)
    return np.kron(conference, np.array([[1.0, 1.0], [1.0, -1.0]])) + np.kron(
        np.eye(modulus + 1), np.array([[1.0, -1.0], [-1.0, -1.0]])
    )


def sylvester_table(length):
    indices = np.arange(length)
    intersection = indices[:, None] & indices[None, :]
    parity = intersection & 1
    for shift in range(1, max(length, 2).bit_length()):
        parity = parity ^ intersection >> shift & 1
    return 1.0 - 2.0 * parity


def local_table():
    table = np.kron(sylvester_table(UNITS // HC), paley_table())
    rows = 4 * np.arange(WORDS)[None, :] + np.arange(4)[:, None]
    out = np.zeros((4, WIDE, UNITS), np.float32)
    out[:, :WORDS] = table[rows]
    return out


def nibble(flipped, k):
    if k == 3:
        return flipped >> 12
    return (flipped << (28 - 4 * k)) >> 28


def hadamard(values):
    step = 1
    while step < len(values):
        values = [
            values[i ^ step] - values[i] if i & step else values[i] + values[i ^ step]
            for i in range(len(values))
        ]
        step *= 2
    return values


def kernel(
    hc_hbm, ts_hbm, w_hbm, cs_hbm, r_hbm, out_ref,
    hc, ts_ref, w, cs_ref, r, codes, gathered, mixed, z, rot, wbf, ts_col,
    sa, sb, ra, rb, ta, tb, fa, fb,
    hc_sem, ts_sem, w_sem, cs_sem, r_sem, g_send, g_recv, z_send, z_recv,
    a_send, a_recv, b_send, b_recv, ta_send, ta_recv, tb_send, tb_recv,
):
    me = lax.axis_index("mp")
    y, x = me // SIDE, me % SIDE

    def at(dy, dx):
        return lax.rem(y + dy, SIDE) * SIDE + lax.rem(x + dx, SIDE)

    def remote(src, dst, send, recv, target):
        return pltpu.make_async_remote_copy(
            src_ref=src, dst_ref=dst, send_sem=send, recv_sem=recv,
            device_id={"mp": target}, device_id_type=MESH,
        )

    barrier = pltpu.get_barrier_semaphore()
    for offset in PEERS:
        pl.semaphore_signal(barrier, inc=1, device_id={"mp": at(*offset)}, device_id_type=MESH)

    load_codes = pltpu.make_async_copy(hc_hbm, hc, hc_sem)
    load_codes.start()
    load_ts = pltpu.make_async_copy(ts_hbm, ts_ref, ts_sem)
    load_ts.start()
    load_cs = pltpu.make_async_copy(cs_hbm, cs_ref, cs_sem)
    load_cs.start()
    rows = UNITS // 4
    load_w = [
        pltpu.make_async_copy(w_hbm.at[pl.ds(i * rows, rows)], w.at[pl.ds(i * rows, rows)], w_sem.at[i])
        for i in range(4)
    ]
    for copy in load_w:
        copy.start()
    load_r = pltpu.make_async_copy(r_hbm, r, r_sem)
    load_r.start()

    load_codes.wait()
    flipped = hc[...] ^ 0x888
    for k in range(4):
        codes[pl.ds(k * T, T), :WORDS] = nibble(flipped, k).astype(F32).astype(BF16)
        codes[pl.ds(k * T, T), WORDS:] = jnp.zeros((T, WIDE - WORDS), BF16)

    pl.semaphore_wait(barrier, len(PEERS))

    def rows_of(device):
        return pl.ds(pl.multiple_of(device * SLICE, SLICE), SLICE)

    gather = []
    for i, offset in enumerate(PEERS):
        target = at(*offset)
        gather.append(remote(codes.at[rows_of(target)], gathered.at[me], g_send.at[i], g_recv.at[i], target))
        gather[-1].start()
    gathered[me] = codes[rows_of(me), :]

    for i, copy in enumerate(load_w):
        copy.wait()

        def unpack(step, carry, i=i):
            at_rows = pl.ds(pl.multiple_of(i * rows + step * 32, 32), 32)
            for c in range(SIDE):
                block = w[at_rows, c * WIDE : (c + 1) * WIDE] ^ 0x888
                for k in range(4):
                    wbf[4 * k + c, at_rows, :] = nibble(block, k).astype(F32).astype(BF16)
            return carry

        lax.fori_loop(0, rows // 32, unpack, 0)
    row_id = lax.broadcasted_iota(jnp.int32, (T, T), 0)
    col_id = lax.broadcasted_iota(jnp.int32, (T, T), 1)
    load_ts.wait()
    scales = jnp.broadcast_to(ts_ref[...].reshape(1, T), (T, T))
    ts_col[...] = jnp.sum(jnp.where(row_id == col_id, scales, 0.0), axis=1, keepdims=True) * (
        1.0 / math.sqrt(FF)
    )

    for copy in gather:
        copy.wait_recv()
    for part in range(SLICE // 16):
        at_rows = pl.ds(part * 16, 16)
        for device, value in enumerate(hadamard([gathered[i, at_rows, :] for i in range(N_MP)])):
            mixed[device, at_rows, :] = value
    back = []
    for i, offset in enumerate(PEERS):
        target = at(*offset)
        back.append(remote(mixed.at[target], z.at[rows_of(me)], z_send.at[i], z_recv.at[i], target))
        back[-1].start()
    z[rows_of(me), :] = mixed[me]

    load_r.wait()
    for copy in back:
        copy.wait_recv()
    total = jnp.dot(z[pl.ds(0, T), :], r[0], preferred_element_type=F32)
    for k in range(1, 4):
        total += jnp.dot(z[pl.ds(k * T, T), :], r[k], preferred_element_type=F32)
    rot[...] = (total * ts_col[...]).astype(BF16)

    first_a, first_b = {}, {}
    for dy, dx in ORDER:
        product = jnp.dot(rot[...], wbf[at(dy, dx)], preferred_element_type=F32).astype(BF16)
        sa[dy, dx] = product[:, :HALF]
        sb[dx, dy] = product[:, HALF:]
        i = 4 * dy + dx
        if dx:
            first_a[dy, dx] = remote(sa.at[dy, dx], ra.at[dy, dx], a_send.at[i], a_recv.at[i], at(0, dx))
            first_a[dy, dx].start()
        if dy:
            first_b[dx, dy] = remote(sb.at[dx, dy], rb.at[dx, dy], b_send.at[i], b_recv.at[i], at(dy, 0))
            first_b[dx, dy].start()

    def summed(own, arrived, copies, major):
        total = own[major, 0].astype(F32)
        for minor in range(1, SIDE):
            copies[major, minor].wait_recv()
            total += arrived[major, minor].astype(F32)
        return total

    second_a, second_b = {}, {}
    for d in (2, 1, 3):
        ta[d] = summed(sa, ra, first_a, d).astype(BF16)
        second_a[d] = remote(ta.at[d], fa.at[d], ta_send.at[d], ta_recv.at[d], at(d, 0))
        second_a[d].start()
        tb[d] = summed(sb, rb, first_b, d).astype(BF16)
        second_b[d] = remote(tb.at[d], fb.at[d], tb_send.at[d], tb_recv.at[d], at(0, d))
        second_b[d].start()
    load_cs.wait()
    scale = cs_ref[...].reshape(1, WIDE)
    total_a = summed(sa, ra, first_a, 0)
    total_b = summed(sb, rb, first_b, 0)
    for d in (2, 1, 3):
        second_a[d].wait_recv()
        total_a += fa[d].astype(F32)
    out_ref[:, :HALF] = (total_a * scale[:, :HALF]).astype(BF16)
    for d in (2, 1, 3):
        second_b[d].wait_recv()
        total_b += fb[d].astype(F32)
    out_ref[:, HALF:] = (total_b * scale[:, HALF:]).astype(BF16)

    for copies in (gather, back, first_a.values(), first_b.values(), second_a.values(), second_b.values()):
        for copy in copies:
            copy.wait_send()


def on_device(hidden_codes, token_scales, weight_codes, column_scales):
    table = jnp.asarray(local_table(), BF16)
    dma = pltpu.SemaphoreType.DMA
    vmem = pl.BlockSpec(memory_space=pltpu.VMEM)
    hbm = pl.BlockSpec(memory_space=pltpu.HBM)
    sums = pltpu.VMEM((SIDE, SIDE, T, HALF), BF16)
    ends = pltpu.VMEM((SIDE, T, HALF), BF16)
    return pl.pallas_call(
        kernel,
        out_shape=jax.ShapeDtypeStruct((T, WIDE), BF16),
        in_specs=[hbm] * 5,
        out_specs=vmem,
        scratch_shapes=[
            pltpu.VMEM((T, WORDS), jnp.int32),
            pltpu.VMEM((T,), F32),
            pltpu.VMEM((UNITS, 4 * WIDE), jnp.int32),
            pltpu.VMEM((WIDE,), F32),
            pltpu.VMEM((4, WIDE, UNITS), BF16),
            pltpu.VMEM((4 * T, WIDE), BF16),
            pltpu.VMEM((N_MP, SLICE, WIDE), BF16),
            pltpu.VMEM((N_MP, SLICE, WIDE), BF16),
            pltpu.VMEM((4 * T, WIDE), BF16),
            pltpu.VMEM((T, UNITS), BF16),
            pltpu.VMEM((N_MP, UNITS, WIDE), BF16),
            pltpu.VMEM((T, 1), F32),
            sums, sums, sums, sums, ends, ends, ends, ends,
            dma, dma, dma((4,)), dma, dma,
            dma((15,)), dma((15,)), dma((15,)), dma((15,)),
            dma((16,)), dma((16,)), dma((16,)), dma((16,)),
            dma((4,)), dma((4,)), dma((4,)), dma((4,)),
        ],
        compiler_params=pltpu.CompilerParams(
            collective_id=0, has_side_effects=True, vmem_limit_bytes=64 * 2**20
        ),
    )(hidden_codes, token_scales, weight_codes, column_scales, table)


def solution(mesh):
    return jax.shard_map(
        on_device,
        mesh=mesh,
        in_specs=(P("dp", "mp"), P("dp"), P("mp", None), P("mp")),
        out_specs=P("dp", "mp"),
        check_vma=False,
    )
```

time: 169 us -> 37.4 us (0.22)
  the two profiles are of different devices: /device:TPU:2 before, /device:TPU:8 now
where the time goes in v1:
time: 37.4 us; the launch traced here: 37.2 us
  Pallas kernels  35.7 us (95%)
  local copies, waits for them, and re-layouts  1.54 us (4%)
    pallas_call x1, Pallas kernels, on_device(): pl.pallas_call(kernel, out_shape=jax.ShapeDtypeStruct((T, WIDE), BF16), i...  35.7 us
    unnamed x1, local copies, waits for them, and re-layouts  1.54 us

profile of v1, /device:TPU:8, one launch (start us, length us, event | category | flops | bytes accessed | tf_op | source)
XLA Modules:
  0.0 37.2 jit_solution(163094150839409320)
XLA Ops:
  0.0 35.7 %shard_map.55 = bf16[192,256]{1,0:T(8,128)(2,1)} custom-call(s32[192,224]{1,0:T(8,128)} %hc_hbm.1, f32[192]{0:T(256)} %ts_hbm.1, s32[896,1024]{1,0:T(8,128)} %w_hbm.1, f32[256]{0:T(256)} %cs_hbm.1, bf16[4,256,896]{2,1,0:T(8,128)(2,1)} %constant.2.clone.r_hbm), custom_call_target="tpu_custom_call" | custom-call | tf_op jit(solution)/shard_map/pallas_call | solution.py:235
  35.7 1.5 %copy.7 = bf16[192,256]{1,0:T(8,128)(2,1)} copy(bf16[192,256]{1,0:T(8,128)(2,1)} %shard_map.55) | data formatting | bytes 196608

commit v2 on v0

v2 whole, which is shorter than its diff:
```python
import math

import jax
import jax.numpy as jnp
import numpy as np
from jax import lax
from jax.experimental import pallas as pl
from jax.experimental.pallas import tpu as pltpu
from jax.sharding import PartitionSpec as P

HC = 28
FF = 14336
SIDE = 4
N_MP = 16
T = 192
CHUNKS = ((0, 96), (96, 96))
WORDS = 224
WIDE = 256
UNITS = 896
HALF = 128
W_PARTS = 4
F32 = jnp.float32
BF16 = jnp.bfloat16
MESH = pl.DeviceIdType.MESH

HOPS = (0, 1, 2, 1)
PEERS = sorted(
    [(ey, ex) for ey in range(SIDE) for ex in range(SIDE) if ey or ex],
    key=lambda o: -(HOPS[o[0]] + HOPS[o[1]]),
)
ORDER = [
    ((1, 2), ""), ((3, 2), ""), ((2, 2), "a2"), ((2, 1), ""), ((2, 3), "b2"),
    ((1, 1), ""), ((3, 1), "a1"), ((1, 3), "b1"), ((3, 3), "a3 b3"),
    ((0, 1), ""), ((0, 2), ""), ((0, 3), ""), ((1, 0), ""), ((2, 0), ""), ((3, 0), ""), ((0, 0), ""),
]


def paley_table():
    modulus = 13
    residues = set((value * value % modulus for value in range(1, modulus)))
    symbols = np.array([0.0] + [1.0 if value in residues else -1.0 for value in range(1, modulus)])
    indices = np.arange(modulus)
    jacobsthal = symbols[(indices[None, :] - indices[:, None]) % modulus]
    first_row = np.concatenate([np.zeros((1, 1)), np.ones((1, modulus))], axis=1)
    other_rows = np.concatenate([np.ones((modulus, 1)), jacobsthal], axis=1)
    conference = np.concatenate([first_row, other_rows], axis=0)
    return np.kron(conference, np.array([[1.0, 1.0], [1.0, -1.0]])) + np.kron(
        np.eye(modulus + 1), np.array([[1.0, -1.0], [-1.0, -1.0]])
    )


def sylvester_table(length):
    indices = np.arange(length)
    intersection = indices[:, None] & indices[None, :]
    parity = intersection & 1
    for shift in range(1, max(length, 2).bit_length()):
        parity = parity ^ intersection >> shift & 1
    return 1.0 - 2.0 * parity


def local_table():
    table = np.kron(sylvester_table(UNITS // HC), paley_table())
    rows = 4 * np.arange(WORDS)[None, :] + np.arange(4)[:, None]
    out = np.zeros((4, WIDE, UNITS), np.float32)
    out[:, :WORDS] = table[rows]
    return out


def nibble(flipped, k):
    if k == 3:
        return flipped >> 12
    return (flipped << (28 - 4 * k)) >> 28


def hadamard(values):
    step = 1
    while step < len(values):
        values = [
            values[i ^ step] - values[i] if i & step else values[i] + values[i ^ step]
            for i in range(len(values))
        ]
        step *= 2
    return values


def other(place, e):
    if e == 1:
        return place + 1 - 2 * lax.rem(place, 2)
    if e == 2:
        return lax.rem(place + 2, SIDE)
    return 3 - place if e else place


class Sum:
    def __init__(self, remote, to_minor, to_major, buffers, sems):
        self.remote, self.to_minor, self.to_major = remote, to_minor, to_major
        self.s, self.r, self.keep, self.t, self.f = buffers
        self.sems = sems
        self.first, self.last = {}, {}

    def put(self, major, minor, value):
        if minor:
            self.s[minor, major] = value
        else:
            self.keep[major] = value

    def start_first(self, minor, group):
        majors, i = (pl.ds(1, 3), minor) if group == "far" else (pl.ds(0, 1), SIDE + minor)
        self.first[minor, group] = self.remote(
            self.s.at[minor, majors], self.r.at[minor, majors], self.sems[0].at[i], self.sems[1].at[i],
            self.to_minor(minor),
        )
        self.first[minor, group].start()

    def own(self, major):
        total = self.keep[major].astype(F32)
        for minor in range(1, SIDE):
            total += self.r[minor, major].astype(F32)
        return total

    def start_last(self):
        for minor in (1, 3, 2):
            self.first[minor, "far"].wait_recv()
        for major in (2, 1, 3):
            self.t[major] = self.own(major).astype(BF16)
            self.last[major] = self.remote(
                self.t.at[major], self.f.at[major], self.sems[2].at[major], self.sems[3].at[major], self.to_major(major)
            )
            self.last[major].start()

    def finish(self):
        for minor in (1, 3, 2):
            self.first[minor, "near"].wait_recv()
        total = self.own(0)
        for major in (1, 3, 2):
            self.last[major].wait_recv()
            total += self.f[major].astype(F32)
        return total

    def copies(self):
        return [*self.first.values(), *self.last.values()]


def kernel(*refs):
    (hc_hbm, ts_hbm, w_hbm, cs_hbm, r_hbm, out_ref), refs = refs[:6], refs[6:]
    (hc, ts_ref, w, cs_ref, r, wbf, ts_col), refs = refs[:7], refs[7:]
    (hc_sem, ts_sem, w_sem, cs_sem, r_sem), refs = refs[:5], refs[5:]
    chunks = [Chunk(start, size, refs[27 * c : 27 * (c + 1)]) for c, (start, size) in enumerate(CHUNKS)]

    me = lax.axis_index("mp")
    y, x = me // SIDE, me % SIDE

    def at(ey, ex):
        return other(y, ey) * SIDE + other(x, ex)

    def remote(src, dst, send, recv, target):
        return pltpu.make_async_remote_copy(
            src_ref=src, dst_ref=dst, send_sem=send, recv_sem=recv,
            device_id={"mp": target}, device_id_type=MESH,
        )

    load_codes = pltpu.make_async_copy(hc_hbm, hc, hc_sem)
    load_codes.start()
    barrier = pltpu.get_barrier_semaphore()
    for offset in PEERS:
        pl.semaphore_signal(barrier, inc=1, device_id={"mp": at(*offset)}, device_id_type=MESH)

    rows = UNITS // W_PARTS
    load_w = [
        pltpu.make_async_copy(w_hbm.at[pl.ds(i * rows, rows)], w.at[pl.ds(i * rows, rows)], w_sem.at[i])
        for i in range(W_PARTS)
    ]
    for copy in load_w:
        copy.start()
    load_ts = pltpu.make_async_copy(ts_hbm, ts_ref, ts_sem)
    load_cs = pltpu.make_async_copy(cs_hbm, cs_ref, cs_sem)
    load_r = pltpu.make_async_copy(r_hbm, r, r_sem)
    load_r.start()
    load_ts.start()
    load_cs.start()

    load_codes.wait()
    for c in chunks:
        flipped = hc[pl.ds(c.start, c.size), :] ^ 0x888
        for k in range(4):
            code = nibble(flipped, k).astype(F32).astype(BF16)
            c.codes[c.of(k), :] = code[:, :HALF]
            c.codes[c.of(4 + k), : WORDS - HALF] = code[:, HALF:]
            c.codes[c.of(4 + k), WORDS - HALF :] = jnp.zeros((c.size, WIDE - WORDS), BF16)

    pl.semaphore_wait(barrier, len(PEERS))

    for c in chunks:
        for i, offset in enumerate(PEERS):
            target = at(*offset)
            c.gather.append(
                remote(c.codes.at[c.slice(target)], c.gathered.at[me], c.g_send.at[i], c.g_recv.at[i], target)
            )
            c.gather[-1].start()
        c.gathered[me] = c.codes[c.slice(me), :]

    def unpack(i):
        load_w[i].wait()

        def some(step, carry):
            at_rows = pl.ds(pl.multiple_of(i * rows + step * 32, 32), 32)
            for column in range(SIDE):
                block = w[at_rows, column * WIDE : (column + 1) * WIDE] ^ 0x888
                for k in range(4):
                    wbf[4 * k + column, at_rows, :] = nibble(block, k).astype(F32).astype(BF16)
            return carry

        lax.fori_loop(0, rows // 32, some, 0)

    for i in range(W_PARTS // 2):
        unpack(i)

    for c in chunks:
        for copy in c.gather:
            copy.wait_recv()
        for part in range(c.rows // 16):
            at_rows = pl.ds(part * 16, 16)
            for device, value in enumerate(hadamard([c.gathered[i, at_rows, :] for i in range(N_MP)])):
                c.mixed[device, at_rows, :] = value
        for i, offset in enumerate(PEERS):
            target = at(*offset)
            c.back.append(remote(c.mixed.at[target], c.z.at[c.slice(me)], c.z_send.at[i], c.z_recv.at[i], target))
            c.back[-1].start()
        c.z[c.slice(me), :] = c.mixed[me]

    for i in range(W_PARTS // 2, W_PARTS):
        unpack(i)
    load_ts.wait()
    row_id = lax.broadcasted_iota(jnp.int32, (T, T), 0)
    col_id = lax.broadcasted_iota(jnp.int32, (T, T), 1)
    scales = jnp.broadcast_to(ts_ref[...].reshape(1, T), (T, T))
    ts_col[...] = jnp.sum(jnp.where(row_id == col_id, scales, 0.0), axis=1, keepdims=True) * (
        1.0 / math.sqrt(FF)
    )
    load_r.wait()
    load_cs.wait()

    for c in chunks:
        for copy in c.back:
            copy.wait_recv()
        total = jnp.zeros((c.size, UNITS), F32)
        for k in range(4):
            some = jnp.concatenate([c.z[c.of(k), :], c.z[c.of(4 + k), :]], axis=1)
            total += jnp.dot(some, r[k], preferred_element_type=F32)
        c.rot[...] = (total * ts_col[pl.ds(c.start, c.size), :]).astype(BF16)

        c.a = Sum(remote, lambda e: at(0, e), lambda e: at(e, 0), c.buffers_a, c.sems_a)
        c.b = Sum(remote, lambda e: at(e, 0), lambda e: at(0, e), c.buffers_b, c.sems_b)
        for (ey, ex), ready in ORDER:
            product = jnp.dot(c.rot[...], wbf[at(ey, ex)], preferred_element_type=F32).astype(BF16)
            c.a.put(ey, ex, product[:, :HALF])
            c.b.put(ex, ey, product[:, HALF:])
            for name in ready.split():
                getattr(c, name[0]).start_first(int(name[1]), "far")
        if c is not chunks[-1]:
            for minor in (2, 1, 3):
                c.a.start_first(minor, "near")
                c.b.start_first(minor, "near")

    for c in chunks:
        c.a.start_last()
        c.b.start_last()
        if c is chunks[-2]:
            for minor in (2, 1, 3):
                chunks[-1].a.start_first(minor, "near")
                chunks[-1].b.start_first(minor, "near")
    scale = cs_ref[...].reshape(1, WIDE)
    for c in chunks:
        out_ref[pl.ds(c.start, c.size), :HALF] = (c.a.finish() * scale[:, :HALF]).astype(BF16)
        out_ref[pl.ds(c.start, c.size), HALF:] = (c.b.finish() * scale[:, HALF:]).astype(BF16)

    for c in chunks:
        for copy in [*c.gather, *c.back, *c.a.copies(), *c.b.copies()]:
            copy.wait_send()


def chunk_scratch(size):
    dma = pltpu.SemaphoreType.DMA
    sliced = pltpu.VMEM((N_MP, size // 2, HALF), BF16)
    stacked = pltpu.VMEM((8 * size, HALF), BF16)
    blocks = pltpu.VMEM((SIDE, SIDE, size, HALF), BF16)
    row = pltpu.VMEM((SIDE, size, HALF), BF16)
    peers = dma((len(PEERS),))
    return [
        stacked, sliced, sliced, stacked, pltpu.VMEM((size, UNITS), BF16),
        *([blocks, blocks, row, row, row] * 2),
        *([peers] * 4),
        *([dma((2 * SIDE,)), dma((2 * SIDE,)), dma((SIDE,)), dma((SIDE,))] * 2),
    ]


class Chunk:
    def __init__(self, start, size, refs):
        self.start, self.size, self.rows = start, size, size // 2
        self.codes, self.gathered, self.mixed, self.z, self.rot = refs[:5]
        self.buffers_a, self.buffers_b = refs[5:10], refs[10:15]
        self.g_send, self.g_recv, self.z_send, self.z_recv = refs[15:19]
        self.sems_a, self.sems_b = refs[19:23], refs[23:27]
        self.gather, self.back = [], []

    def of(self, k):
        return pl.ds(k * self.size, self.size)

    def slice(self, device):
        return pl.ds(pl.multiple_of(device * self.rows, self.rows), self.rows)


def on_device(hidden_codes, token_scales, weight_codes, column_scales):
    operands = (hidden_codes, token_scales, weight_codes, column_scales, jnp.asarray(local_table(), BF16))
    dma = pltpu.SemaphoreType.DMA
    hbm = pl.BlockSpec(memory_space=pltpu.HBM)
    return pl.pallas_call(
        kernel,
        out_shape=jax.ShapeDtypeStruct((T, WIDE), BF16),
        in_specs=[hbm] * 5,
        out_specs=pl.BlockSpec(memory_space=pltpu.VMEM),
        scratch_shapes=[
            pltpu.VMEM((T, WORDS), jnp.int32),
            pltpu.VMEM((T,), F32),
            pltpu.VMEM((UNITS, 4 * WIDE), jnp.int32),
            pltpu.VMEM((WIDE,), F32),
            pltpu.VMEM((4, WIDE, UNITS), BF16),
            pltpu.VMEM((N_MP, UNITS, WIDE), BF16),
            pltpu.VMEM((T, 1), F32),
            dma, dma, dma((W_PARTS,)), dma, dma,
            *[ref for _, size in CHUNKS for ref in chunk_scratch(size)],
        ],
        compiler_params=pltpu.CompilerParams(
            collective_id=0, has_side_effects=True, vmem_limit_bytes=48 * 2**20
        ),
    )(*[pltpu.with_memory_space_constraint(operand, pltpu.HBM) for operand in operands])


def solution(mesh):
    return jax.shard_map(
        on_device,
        mesh=mesh,
        in_specs=(P("dp", "mp"), P("dp"), P("mp", None), P("mp")),
        out_specs=P("dp", "mp"),
        check_vma=False,
    )
```

time: 169 us -> 34.6 us (0.20)
  the two profiles are of different devices: /device:TPU:2 before, /device:TPU:8 now
where the time goes in v2:
time: 34.6 us; the launch traced here: 34.4 us
  Pallas kernels  33.8 us (98%)
  local copies, waits for them, and re-layouts  0.64 us (2%)
    pallas_call x1, Pallas kernels, on_device(): pl.pallas_call(kernel, out_shape=jax.ShapeDtypeStruct((T, WIDE), BF16), i...  33.8 us

profile of v2, /device:TPU:8, one launch (start us, length us, event | category | flops | bytes accessed | tf_op | source)
XLA Modules:
  0.0 34.4 jit_solution(13334142613086528676)
XLA Ops:
  0.0 33.8 %shard_map.55 = bf16[192,256]{1,0:T(8,128)(2,1)S(1)} custom-call(s32[192,224]{1,0:T(8,128)} %refs_0_.1, f32[192]{0:T(256)} %refs_1_.1, s32[896,1024]{1,0:T(8,128)} %refs_2_.1, f32[256]{0:T(256)} %refs_3_.1, bf16[4,256,896]{2,1,0:T(8,128)(2,1)} %constant.2.clone.refs_4_), custom_call_target="tpu_custom_call" | custom-call | tf_op jit(solution)/shard_map/pallas_call | solution.py:317
  33.8 0.6 %copy.7 = bf16[192,256]{1,0:T(8,128)(2,1)} copy(bf16[192,256]{1,0:T(8,128)(2,1)S(1)} %shard_map.55) | data formatting | bytes 196608

commit v3 on v2

--- a/solution.py
+++ b/solution.py
@@ -14,6 +14,8 @@
 N_MP = 16
 T = 192
 CHUNKS = ((0, 96), (96, 96))
+GATHER = ((0, 0), (0, 0))
+NEAR = ((0, 0), (2, 2))
 WORDS = 224
 WIDE = 256
 UNITS = 896
@@ -91,12 +93,15 @@
     return 3 - place if e else place
 
 
+def wait_bytes(ref, sem):
+    pltpu.make_async_copy(ref, ref, sem).wait()
+
+
 class Sum:
     def __init__(self, remote, to_minor, to_major, buffers, sems):
         self.remote, self.to_minor, self.to_major = remote, to_minor, to_major
         self.s, self.r, self.keep, self.t, self.f = buffers
-        self.sems = sems
-        self.first, self.last = {}, {}
+        self.first_send, self.far, self.near, self.last_send, self.last = (sems.at[i] for i in range(5))
 
     def put(self, major, minor, value):
         if minor:
@@ -104,13 +109,13 @@
         else:
             self.keep[major] = value
 
-    def start_first(self, minor, group):
-        majors, i = (pl.ds(1, 3), minor) if group == "far" else (pl.ds(0, 1), SIDE + minor)
-        self.first[minor, group] = self.remote(
-            self.s.at[minor, majors], self.r.at[minor, majors], self.sems[0].at[i], self.sems[1].at[i],
+    def make_first(self, minor, group):
+        far = group == "far"
+        majors = pl.ds(1, 3) if far else pl.ds(0, 1)
+        return self.remote(
+            self.s.at[minor, majors], self.r.at[minor, majors], self.first_send, self.far if far else self.near,
             self.to_minor(minor),
         )
-        self.first[minor, group].start()
 
     def own(self, major):
         total = self.keep[major].astype(F32)
@@ -119,33 +124,33 @@
         return total
 
     def start_last(self):
-        for minor in (1, 3, 2):
-            self.first[minor, "far"].wait_recv()
+        wait_bytes(self.r.at[pl.ds(1, 3), pl.ds(1, 3)], self.far)
         for major in (2, 1, 3):
             self.t[major] = self.own(major).astype(BF16)
-            self.last[major] = self.remote(
-                self.t.at[major], self.f.at[major], self.sems[2].at[major], self.sems[3].at[major], self.to_major(major)
-            )
-            self.last[major].start()
+            self.remote(
+                self.t.at[major], self.f.at[major], self.last_send, self.last, self.to_major(major)
+            ).start()
 
     def finish(self):
-        for minor in (1, 3, 2):
-            self.first[minor, "near"].wait_recv()
+        wait_bytes(self.r.at[pl.ds(1, 3), pl.ds(0, 1)], self.near)
         total = self.own(0)
+        wait_bytes(self.f.at[pl.ds(1, 3)], self.last)
         for major in (1, 3, 2):
-            self.last[major].wait_recv()
             total += self.f[major].astype(F32)
         return total
 
-    def copies(self):
-        return [*self.first.values(), *self.last.values()]
+    def wait_first_sends(self):
+        wait_bytes(self.s.at[pl.ds(1, 3)], self.first_send)
+
+    def wait_last_sends(self):
+        wait_bytes(self.t.at[pl.ds(1, 3)], self.last_send)
 
 
 def kernel(*refs):
     (hc_hbm, ts_hbm, w_hbm, cs_hbm, r_hbm, out_ref), refs = refs[:6], refs[6:]
     (hc, ts_ref, w, cs_ref, r, wbf, ts_col), refs = refs[:7], refs[7:]
     (hc_sem, ts_sem, w_sem, cs_sem, r_sem), refs = refs[:5], refs[5:]
-    chunks = [Chunk(start, size, refs[27 * c : 27 * (c + 1)]) for c, (start, size) in enumerate(CHUNKS)]
+    chunks = [Chunk(start, size, refs[18 * c : 18 * (c + 1)]) for c, (start, size) in enumerate(CHUNKS)]
 
     me = lax.axis_index("mp")
     y, x = me // SIDE, me % SIDE
@@ -190,14 +195,28 @@
 
     pl.semaphore_wait(barrier, len(PEERS))
 
-    for c in chunks:
-        for i, offset in enumerate(PEERS):
+    core = lax.rem(lax.axis_index("dp"), 2)
+
+    def start_at(point, points, copies):
+        def start():
+            for copy in copies:
+                copy.start()
+
+        if points == (point, point):
+            start()
+        elif point in points:
+            pl.when(core == points.index(point))(start)
+
+    def start_gather(point):
+        for c, points in zip(chunks, GATHER):
+            start_at(point, points, c.gather)
+
+    for c in chunks:
+        for offset in PEERS:
             target = at(*offset)
-            c.gather.append(
-                remote(c.codes.at[c.slice(target)], c.gathered.at[me], c.g_send.at[i], c.g_recv.at[i], target)
-            )
-            c.gather[-1].start()
+            c.gather.append(remote(c.codes.at[c.slice(target)], c.gathered.at[me], c.g_send, c.g_recv, target))
         c.gathered[me] = c.codes[c.slice(me), :]
+    start_gather(0)
 
     def unpack(i):
         load_w[i].wait()
@@ -214,18 +233,17 @@
 
     for i in range(W_PARTS // 2):
         unpack(i)
-
-    for c in chunks:
-        for copy in c.gather:
-            copy.wait_recv()
+        start_gather(i + 1)
+
+    for c in chunks:
+        wait_bytes(c.gathered.at[pl.ds(0, len(PEERS))], c.g_recv)
         for part in range(c.rows // 16):
             at_rows = pl.ds(part * 16, 16)
             for device, value in enumerate(hadamard([c.gathered[i, at_rows, :] for i in range(N_MP)])):
                 c.mixed[device, at_rows, :] = value
-        for i, offset in enumerate(PEERS):
+        for offset in PEERS:
             target = at(*offset)
-            c.back.append(remote(c.mixed.at[target], c.z.at[c.slice(me)], c.z_send.at[i], c.z_recv.at[i], target))
-            c.back[-1].start()
+            remote(c.mixed.at[target], c.z.at[c.slice(me)], c.z_send, c.z_recv, target).start()
         c.z[c.slice(me), :] = c.mixed[me]
 
     for i in range(W_PARTS // 2, W_PARTS):
@@ -240,9 +258,12 @@
     load_r.wait()
     load_cs.wait()
 
-    for c in chunks:
-        for copy in c.back:
-            copy.wait_recv()
+    def start_near(point):
+        for c, points in zip(chunks, NEAR):
+            start_at(point, points, getattr(c, "near", ()))
+
+    for c in chunks:
+        wait_bytes(c.z.at[pl.ds(0, len(PEERS) * c.rows)], c.z_recv)
         total = jnp.zeros((c.size, UNITS), F32)
         for k in range(4):
             some = jnp.concatenate([c.z[c.of(k), :], c.z[c.of(4 + k), :]], axis=1)
@@ -256,27 +277,28 @@
             c.a.put(ey, ex, product[:, :HALF])
             c.b.put(ex, ey, product[:, HALF:])
             for name in ready.split():
-                getattr(c, name[0]).start_first(int(name[1]), "far")
-        if c is not chunks[-1]:
-            for minor in (2, 1, 3):
-                c.a.start_first(minor, "near")
-                c.b.start_first(minor, "near")
-
+                getattr(c, name[0]).make_first(int(name[1]), "far").start()
+        c.near = [half.make_first(minor, "near") for minor in (2, 1, 3) for half in (c.a, c.b)]
+        start_near(chunks.index(c))
+
+    for c in chunks:
+        wait_bytes(c.gathered.at[pl.ds(0, len(PEERS))], c.g_send)
+        wait_bytes(c.z.at[pl.ds(0, len(PEERS) * c.rows)], c.z_send)
     for c in chunks:
         c.a.start_last()
         c.b.start_last()
-        if c is chunks[-2]:
-            for minor in (2, 1, 3):
-                chunks[-1].a.start_first(minor, "near")
-                chunks[-1].b.start_first(minor, "near")
+        start_near(len(chunks) + chunks.index(c))
+    for c in chunks:
+        c.a.wait_first_sends()
+        c.b.wait_first_sends()
     scale = cs_ref[...].reshape(1, WIDE)
     for c in chunks:
         out_ref[pl.ds(c.start, c.size), :HALF] = (c.a.finish() * scale[:, :HALF]).astype(BF16)
         out_ref[pl.ds(c.start, c.size), HALF:] = (c.b.finish() * scale[:, HALF:]).astype(BF16)
 
     for c in chunks:
-        for copy in [*c.gather, *c.back, *c.a.copies(), *c.b.copies()]:
-            copy.wait_send()
+        c.a.wait_last_sends()
+        c.b.wait_last_sends()
 
 
 def chunk_scratch(size):
@@ -285,12 +307,10 @@
     stacked = pltpu.VMEM((8 * size, HALF), BF16)
     blocks = pltpu.VMEM((SIDE, SIDE, size, HALF), BF16)
     row = pltpu.VMEM((SIDE, size, HALF), BF16)
-    peers = dma((len(PEERS),))
     return [
         stacked, sliced, sliced, stacked, pltpu.VMEM((size, UNITS), BF16),
         *([blocks, blocks, row, row, row] * 2),
-        *([peers] * 4),
-        *([dma((2 * SIDE,)), dma((2 * SIDE,)), dma((SIDE,)), dma((SIDE,))] * 2),
+        dma((4,)), dma((5,)), dma((5,)),
     ]
 
 
@@ -299,9 +319,9 @@
         self.start, self.size, self.rows = start, size, size // 2
         self.codes, self.gathered, self.mixed, self.z, self.rot = refs[:5]
         self.buffers_a, self.buffers_b = refs[5:10], refs[10:15]
-        self.g_send, self.g_recv, self.z_send, self.z_recv = refs[15:19]
-        self.sems_a, self.sems_b = refs[19:23], refs[23:27]
-        self.gather, self.back = [], []
+        self.g_send, self.g_recv, self.z_send, self.z_recv = (refs[15].at[i] for i in range(4))
+        self.sems_a, self.sems_b = refs[16:18]
+        self.gather = []
 
     def of(self, k):
         return pl.ds(k * self.size, self.size)

time: 34.6 us -> 32.7 us (0.945)
  Pallas kernels: 33.8 us -> 31.9 us
    pallas_call x1, Pallas kernels: 33.8 us -> 31.9 us  [on_device(): pl.pallas_call(kernel, out_shape=jax.ShapeDtypeStruct((T, WIDE), BF16), i...]
where the time goes in v3:
time: 32.7 us; the launch traced here: 32.6 us
  Pallas kernels  31.9 us (98%)
  local copies, waits for them, and re-layouts  0.64 us (2%)
    pallas_call x1, Pallas kernels, on_device(): pl.pallas_call(kernel, out_shape=jax.ShapeDtypeStruct((T, WIDE), BF16), i...  31.9 us

profile of v3, /device:TPU:8, one launch (start us, length us, event | category | flops | bytes accessed | tf_op | source)
XLA Modules:
  0.0 32.6 jit_solution(18275118475889849916)
XLA Ops:
  0.0 31.9 %shard_map.55 = bf16[192,256]{1,0:T(8,128)(2,1)S(1)} custom-call(s32[192,224]{1,0:T(8,128)} %refs_0_.1, f32[192]{0:T(256)} %refs_1_.1, s32[896,1024]{1,0:T(8,128)} %refs_2_.1, f32[256]{0:T(256)} %refs_3_.1, bf16[4,256,896]{2,1,0:T(8,128)(2,1)} %constant.2.clone.refs_4_), custom_call_target="tpu_custom_call" | custom-call | tf_op jit(solution)/shard_map/pallas_call | solution.py:337
  31.9 0.6 %copy.7 = bf16[192,256]{1,0:T(8,128)(2,1)} copy(bf16[192,256]{1,0:T(8,128)(2,1)S(1)} %shard_map.55) | data formatting | bytes 196608

commit v4 on v3

--- a/solution.py
+++ b/solution.py
@@ -31,9 +31,8 @@
     key=lambda o: -(HOPS[o[0]] + HOPS[o[1]]),
 )
 ORDER = [
-    ((1, 2), ""), ((3, 2), ""), ((2, 2), "a2"), ((2, 1), ""), ((2, 3), "b2"),
-    ((1, 1), ""), ((3, 1), "a1"), ((1, 3), "b1"), ((3, 3), "a3 b3"),
-    ((0, 1), ""), ((0, 2), ""), ((0, 3), ""), ((1, 0), ""), ((2, 0), ""), ((3, 0), ""), ((0, 0), ""),
+    (2, 2), (1, 2), (2, 1), (3, 2), (2, 3), (1, 1), (3, 1), (1, 3), (3, 3),
+    (0, 1), (0, 2), (0, 3), (1, 0), (2, 0), (3, 0), (0, 0),
 ]
 
 
@@ -109,9 +108,9 @@
         else:
             self.keep[major] = value
 
-    def make_first(self, minor, group):
-        far = group == "far"
-        majors = pl.ds(1, 3) if far else pl.ds(0, 1)
+    def make_first(self, minor, major):
+        far = major > 0
+        majors = pl.ds(major, 1)
         return self.remote(
             self.s.at[minor, majors], self.r.at[minor, majors], self.first_send, self.far if far else self.near,
             self.to_minor(minor),
@@ -272,13 +271,14 @@
 
         c.a = Sum(remote, lambda e: at(0, e), lambda e: at(e, 0), c.buffers_a, c.sems_a)
         c.b = Sum(remote, lambda e: at(e, 0), lambda e: at(0, e), c.buffers_b, c.sems_b)
-        for (ey, ex), ready in ORDER:
+        for ey, ex in ORDER:
             product = jnp.dot(c.rot[...], wbf[at(ey, ex)], preferred_element_type=F32).astype(BF16)
             c.a.put(ey, ex, product[:, :HALF])
             c.b.put(ex, ey, product[:, HALF:])
-            for name in ready.split():
-                getattr(c, name[0]).make_first(int(name[1]), "far").start()
-        c.near = [half.make_first(minor, "near") for minor in (2, 1, 3) for half in (c.a, c.b)]
+            if ey and ex:
+                c.a.make_first(ex, ey).start()
+                c.b.make_first(ey, ex).start()
+        c.near = [half.make_first(minor, 0) for minor in (2, 1, 3) for half in (c.a, c.b)]
         start_near(chunks.index(c))
 
     for c in chunks:

time: 32.7 us -> 33.3 us (1.018)
  the two profiles are of different devices: /device:TPU:8 before, /device:TPU:416 now
where the time goes in v4:
time: 33.3 us; the launch traced here: 33.2 us
  Pallas kernels  32.6 us (98%)
  local copies, waits for them, and re-layouts  0.64 us (2%)
    pallas_call x1, Pallas kernels, on_device(): pl.pallas_call(kernel, out_shape=jax.ShapeDtypeStruct((T, WIDE), BF16), i...  32.6 us

profile of v4, /device:TPU:416, one launch (start us, length us, event | category | flops | bytes accessed | tf_op | source)
XLA Modules:
  0.0 33.2 jit_solution(5013313877325281631)
XLA Ops:
  0.0 32.6 %shard_map.55 = bf16[192,256]{1,0:T(8,128)(2,1)S(1)} custom-call(s32[192,224]{1,0:T(8,128)} %refs_0_.1, f32[192]{0:T(256)} %refs_1_.1, s32[896,1024]{1,0:T(8,128)} %refs_2_.1, f32[256]{0:T(256)} %refs_3_.1, bf16[4,256,896]{2,1,0:T(8,128)(2,1)} %constant.2.clone.refs_4_), custom_call_target="tpu_custom_call" | custom-call | tf_op jit(solution)/shard_map/pallas_call | solution.py:337
  32.6 0.6 %copy.7 = bf16[192,256]{1,0:T(8,128)(2,1)} copy(bf16[192,256]{1,0:T(8,128)(2,1)S(1)} %shard_map.55) | data formatting | bytes 196608
